TPU v7x, 256 devices: a whole 4x4x8 slice. The times are simulated.
256 devices in a mesh: row: 64 (over y_hi, x, z), head: 4 (over y_lo, core).
Axes of the slice: x: 4, y: 4 (y_hi: 2, y_lo: 2; y = y_hi * 2 + y_lo), z: 8, core: 2. Of those that a mesh axis runs over, the one named last changes fastest.
Arguments:
- pair: float32 [1024, 1024, 128], P('row', 'head'), may hold values from -6 to 6
- token_mask: int32 [1024], replicated, may hold values from 0 to 1, as said below
- ln_gain: float32 [128], replicated, may hold values from 0.25 to 1.75
- ln_shift: float32 [128], replicated, may hold values from -3 to 3
- w_qkvg: bfloat16 [128, 512], P(None, 'head'), may hold values from -0.5 to 0.5
- w_bias: bfloat16 [128, 4], replicated, may hold values from -0.5 to 0.5
- gate_shift: float32 [128], P('head'), may hold values from -4 to 4
- w_out: bfloat16 [128, 128], P('head'), may hold values from -0.5 to 0.5
- out_shift: float32 [128], replicated, may hold values from -4 to 4
Outputs:
- update: float32 [1024, 1024, 128], P('row', 'head')
Inputs may be any that keep to these rules, and one draw needn't show every extreme that they name: `token_mask`: 1 for the first tokens and 0 for the rest, with at least 512 ones and at least one 0.
All inputs are finite; a program needn't handle non-finite values.
Results may differ from a plain program's by a relative error of at most 0.0055.
Values may be sent and summed in bfloat16 or wider, within the bound.
No kernel may reach another device: no remote copies, remote signals or barrier semaphores. Data moves between devices by JAX's collectives and lax.ppermute only.
A program may use at most 64 MiB of HBM per device.

v0:
```python
import math

import jax
import jax.numpy as jnp
from jax import lax
from jax.sharding import PartitionSpec as P


def layer_norm(values, gain, shift):
    mean = jnp.mean(values, axis=-1, keepdims=True)
    centered = values - mean
    var = jnp.mean(centered * centered, axis=-1, keepdims=True)
    return centered / jnp.sqrt(var + 1e-05) * gain + shift


def local(pair, token_mask, ln_gain, ln_shift, w_qkvg, w_bias, gate_shift, w_out, out_shift):
    rows, local_cols, chans = pair.shape
    normed = layer_norm(pair, ln_gain, ln_shift).astype(jnp.bfloat16)
    local_bias = jnp.einsum(
        "ijc,ch->hij", normed, w_bias, preferred_element_type=jnp.float32
    ).astype(jnp.bfloat16)
    head_bias = lax.all_to_all(local_bias, "head", split_axis=0, concat_axis=2, tiled=True)[0]
    total = head_bias.shape[1]
    full_rows = lax.all_gather(normed, "head", axis=1, tiled=True)
    proj = jnp.dot(full_rows.reshape(-1, chans), w_qkvg, preferred_element_type=jnp.float32)
    proj = proj.astype(jnp.bfloat16).reshape(rows, total, w_qkvg.shape[1])
    width = proj.shape[2] // 4
    query = proj[:, :, 0:width]
    keys = proj[:, :, width : 2 * width]
    values = proj[:, :, 2 * width : 3 * width]
    gate_raw = proj[:, :, 3 * width : 4 * width]
    key_add = jnp.where(token_mask == 1, 0.0, -1000000000.0).astype(jnp.float32)
    scale = 1.0 / math.sqrt(width)
    initial = jnp.zeros((rows, total, width), jnp.float32)
    piece = lax.all_gather(head_bias, "row", axis=0, tiled=True)
    count = piece.shape[0]
    step_rows = math.gcd(count, 32)

    def inner(index, acc):
        offset = index * step_rows
        bias_part = lax.dynamic_slice_in_dim(piece, offset, step_rows, 0).astype(jnp.float32)
        query_part = lax.dynamic_slice_in_dim(query, offset, step_rows, 1)
        scores = (
            jnp.einsum("ijc,ikc->ijk", query_part, keys, preferred_element_type=jnp.float32) * scale
        )
        scores = scores + bias_part[None] + key_add
        weights = jax.nn.softmax(scores, axis=-1).astype(jnp.bfloat16)
        part_out = jnp.einsum("ijk,ikc->ijc", weights, values, preferred_element_type=jnp.float32)
        return lax.dynamic_update_slice_in_dim(acc, part_out, offset, 1)

    attended = lax.fori_loop(0, count // step_rows, inner, initial)
    gated = (jax.nn.sigmoid(gate_raw.astype(jnp.float32) + gate_shift) * attended).astype(
        jnp.bfloat16
    )
    partial_out = jnp.dot(gated.reshape(-1, width), w_out, preferred_element_type=jnp.float32)
    partial_out = partial_out.reshape(rows, total, chans)
    mixed = lax.psum_scatter(
        partial_out.astype(jnp.bfloat16), "head", scatter_dimension=1, tiled=True
    ).astype(jnp.float32)
    return mixed + out_shift


def solution(mesh):
    placed = (
        P("row", "head", None),
        P(),
        P(),
        P(),
        P(None, "head"),
        P(),
        P("head"),
        P("head", None),
        P(),
    )
    return jax.shard_map(
        local, mesh=mesh, in_specs=placed, out_specs=P("row", "head", None), check_vma=False
    )
```

profile of v0, /device:TPU:1, one launch (start us, length us, event | category | flops | bytes accessed | tf_op | source)
XLA Modules:
  0.0 520.6 jit_solution(735047392880219054)
XLA Ops:
  14.1 8.8 %all_to_all.15 = bf16[4,16,256]{2,1,0:T(8,128)(2,1)S(1)} all-to-all(bf16[4,16,256]{2,1,0:T(8,128)(2,1)S(1)} %copy.19), channel_id=1, replica_groups=mesh['row'=64,'head'=4] {'head'}, dimensions={0} | all-to-all | bytes 65536 | tf_op jit(solution)/shard_map/all_to_all | solution.py:22
  23.6 42.3 %all-gather.3.cloned.1.call-done = bf16[16,1024,128]{2,1,0:T(8,128)(2,1)} async-done(((bf16[16,256,128]{2,1,0:T(8,128)(2,1)}), bf16[16,1024,128]{2,1,0:T(8,128)(2,1)}) %all-gather.3.cloned.1.call-update) | async-done | bytes 4194320 | tf_op jit(solution)/shard_map/all_gather | solution.py:24
  65.9 3.4 convolution_convert_fusion
  69.3 7.7 %fusion.27 = (bf16[16,1024,32]{2,1,0:T(8,128)(2,1)}, bf16[16,1024,32]{2,1,0:T(8,128)(2,1)}, bf16[16,1024,32]{2,1,0:T(8,128)(2,1)}, bf16[16,1024,32]{2,1,0:T(8,128)(2,1)}) fusion(bf16[16,1024,128]{2,1,0:T(8,128)(2,1)S(1)} %bitcast.25), kind=kLoop, calls=%fused_computation.32 | loop fusion | bytes 8388608 | tf_op jit(solution)/shard_map/slice | solution.py:31
  77.0 3.5 copy.23
  80.5 4.6 copy.24
  85.1 99.2 %all-gather.5.cloned.1.call-done = bf16[1024,1024]{1,0:T(8,128)(2,1)} async-done(((bf16[16,1024]{1,0:T(8,128)(2,1)}), bf16[1024,1024]{1,0:T(8,128)(2,1)}) %all-gather.5.cloned.1.call-update) | async-done | bytes 2097168 | tf_op jit(solution)/shard_map/all_gather | solution.py:35
  184.6 271.3 %while.13 = (s32[]{:T(128)}, f32[16,1024,32]{1,2,0:T(8,128)S(1)}, bf16[16,1024,32]{2,1,0:T(8,128)(2,1)}, bf16[16,1024,32]{1,2,0:T(8,128)(2,1)S(1)}, bf16[1024,10...) while((s32[]{:T(128)}, f32[16,1024,32]{1,2,0:T(8,128)S(1)}, ...), condition=%wide.region_5.6_spmd, body=%wide.region_2.5_spmd.sunk | while | flops 70812672 | bytes 6955175 | solution.py:51
  185.4 3.0 fusion.41
  192.2 3.0 fusion.41
  201.3 3.0 fusion.41
  226.2 3.0 fusion.41
  253.4 3.0 fusion.41
  269.2 3.0 fusion.41
  321.3 3.0 fusion.41
  328.1 3.0 fusion.41
  355.3 3.0 fusion.41
  362.1 3.0 fusion.41
  389.3 3.0 fusion.41
  405.1 3.0 fusion.41
  438.9 3.0 fusion.41
  455.9 3.5 copy.22
  459.4 3.4 convolution_convert_fusion.1
  462.8 48.5 %reduce-scatter.2.cloned.1.call-done = bf16[16,256,128]{2,1,0:T(8,128)(2,1)} async-done(((bf16[16,1024,128]{2,1,0:T(8,128)(2,1)}), bf16[16,256,128]{2,1,0:T(8,128)(2,1)}) %reduce-scatter.2.cloned.1.call-update) | async-done | bytes 1048592 | tf_op jit(solution)/shard_map/reduce_scatter | solution.py:57
  (151 shorter events, 242.5 us)
Async XLA Ops:
  6.5 59.3 %copy-start = (bf16[128,128]{1,0:T(8,128)(2,1)S(1)}, bf16[128,128]{1,0:T(8,128)(2,1)}, u32[]{:S(2)}) copy-start(bf16[128,128]{1,0:T(8,128)(2,1)} %param.15) | copy-start | bytes 98308
  6.5 2.4 copy-start.1
  6.5 3.7 copy-start.5
  6.5 3.8 copy-start.4
  6.5 59.3 %all-gather.3.cloned.1.call-start = ((), (), s32[]{:S(2)}) async-start(), calls=%async_computation.2 | async-start | bytes 5242880 | tf_op jit(solution)/shard_map/all_gather | solution.py:24
  10.3 2.1 copy-start.3
  10.3 13.2 %copy-start.2 = (s32[1024]{0:T(1024)S(1)}, s32[1024]{0:T(1024)}, u32[]{:S(2)}) copy-start(s32[1024]{0:T(1024)} %param.12) | copy-start | bytes 12292
  12.4 171.9 %all-gather.5.cloned.1.call-start = ((), (), s32[]{:S(2)}) async-start(), calls=%async_computation.3 | async-start | bytes 2129920 | tf_op jit(solution)/shard_map/all_gather | solution.py:35
  23.5 487.8 %reduce-scatter.2.cloned.1.call-start = ((), (), s32[]{:S(2)}) async-start(), calls=%async_computation.4 | async-start | bytes 5242880 | tf_op jit(solution)/shard_map/reduce_scatter | solution.py:57
  455.9 3.5 copy-start.7
  455.9 3.5 copy-start.8
  462.8 48.5 %copy-start.6 = (f32[128]{0:T(128)S(1)}, f32[128]{0:T(128)}, u32[]{:S(2)}) copy-start(f32[128]{0:T(128)} %param.19) | copy-start | bytes 1540
Sparse Core Ops, SparseCore 0:
  12.5 53.3 all-gather.2
  69.6 114.6 all-gather.4
  462.9 48.3 reduce-scatter.1
where the time goes:
time: 523 us; the launch traced here: 521 us
  waiting for transfers between devices  190 us (36%)
  matrix products  179 us (34%)
  local copies, waits for them, and re-layouts  92.4 us (18%)
  other arithmetic  35.8 us (7%)
  between operations  13.3 us (3%)
  blocking collectives  8.76 us (2%)
    all_gather x1, waiting for transfers between devices, local(): piece = lax.all_gather(head_bias, 'row', axis=0, tiled=True)  99.2 us
    sub x32, matrix products, inner(): weights = jax.nn.softmax(scores, axis=-1).astype(jnp.bfloat16)  96 us
    dot_general x32, matrix products, inner(): jnp.einsum('ijk,ikc->ijc', weights, values, preferred_element_type=jnp.fl...  74.8 us
    dynamic_update_slice x32, local copies, waits for them, and re-layouts, inner(): return lax.dynamic_update_slice_in_dim(acc, part_out, offset, 1)  72.2 us
    reduce_scatter x1, waiting for transfers between devices, local(): lax.psum_scatter(partial_out.astype(jnp.bfloat16), 'head', scatter_dimens...  48.5 us
    all_gather x1, waiting for transfers between devices, local(): full_rows = lax.all_gather(normed, 'head', axis=1, tiled=True)  42.3 us
    convert_element_type x32, other arithmetic, inner(): lax.dynamic_slice_in_dim(piece, offset, step_rows, 0).astype(jnp.float32)  27.4 us
    unnamed x22, local copies, waits for them, and re-layouts  12.2 us
  transfers between devices with their start and end apart: 3, of which 3 were waited for; matrix products, arithmetic and copies ran while one was open for 4% of the time, Pallas kernels for 0%

commit v1 on v0

v1 whole, which is shorter than its diff:
```python
import functools
import math

import jax
import jax.numpy as jnp
import numpy as np
from jax import lax
from jax.experimental import pallas as pl
from jax.experimental.pallas import tpu as pltpu
from jax.sharding import PartitionSpec as P

bf16 = jnp.bfloat16
f32 = jnp.float32
LOG2E = math.log2(math.e)
LIMIT = 80.0
VMEM = 48 * 2**20
DIMS = (2, 2, 2, 2, 4, 2, 2)


def dot(a, b):
    return jnp.dot(a, b, preferred_element_type=f32)


def dot_nt(a, b):
    return lax.dot_general(a, b, (((1,), (1,)), ((), ())), preferred_element_type=f32)


def send(value, where):
    pairs = []
    for index in range(256):
        spot = [int(v) for v in np.unravel_index(index, DIMS)]
        pairs.append((index, int(np.ravel_multi_index(where(*spot), DIMS))))
    return lax.ppermute(value, ("row", "head"), pairs)


def to_core(yh, xh, xl, zh, zl, yl, c):
    return yh, xh, xl, zh, zl, yl, 1 - c


def to_chip(yh, xh, xl, zh, zl, yl, c):
    return yh, xh, xl, zh, zl, 1 - yl, c


def to_both(yh, xh, xl, zh, zl, yl, c):
    return yh, xh, xl, zh, zl, 1 - yl, 1 - c


def spread(dy, dz):
    def where(yh, xh, xl, zh, zl, yl, c):
        return yl ^ dy, c, xl, zh ^ dz, zl, yh, xh

    return where


def along_z(step):
    def where(yh, xh, xl, zh, zl, yl, c):
        z = (zh * 4 + zl + step) % 8
        return yh, xh, xl, z // 4, z % 4, yl, c

    return where


def along_x(step):
    def where(yh, xh, xl, zh, zl, yl, c):
        x = (xh * 2 + xl + step) % 4
        return yh, x // 2, x % 2, zh, zl, yl, c

    return where


def norm_kernel(pair, gain, shift, wb, normed, chunk, rows):
    step = pl.program_id(0)
    count = pair.shape[0]
    x = pair[...]
    mean = jnp.mean(x, axis=-1, keepdims=True)
    centered = x - mean
    var = jnp.mean(centered * centered, axis=-1, keepdims=True)
    n = (centered * lax.rsqrt(var + 1e-05) * gain[...] + shift[...]).astype(bf16)
    normed[...] = n
    for ii in range(count):
        t = dot_nt(wb[...], n[ii])
        for h in range(4):
            rows[h, pl.ds(step * count + ii, 1), :] = t[h : h + 1]

    @pl.when(step == pl.num_programs(0) - 1)
    def _():
        chunk[...] = rows[...].astype(bf16)


def norm_call(pair, gain, shift, wb):
    n, cols, chans = pair.shape
    per = 4
    return pl.pallas_call(
        norm_kernel,
        grid=(n // per,),
        in_specs=[
            pl.BlockSpec((per, cols, chans), lambda i: (i, 0, 0)),
            pl.BlockSpec((1, chans), lambda i: (0, 0)),
            pl.BlockSpec((1, chans), lambda i: (0, 0)),
            pl.BlockSpec((16, chans), lambda i: (0, 0)),
        ],
        out_specs=[
            pl.BlockSpec((per, cols, chans), lambda i: (i, 0, 0)),
            pl.BlockSpec((4, n, cols), lambda i: (0, 0, 0)),
        ],
        out_shape=[
            jax.ShapeDtypeStruct((n, cols, chans), bf16),
            jax.ShapeDtypeStruct((4, n, cols), bf16),
        ],
        scratch_shapes=[pltpu.VMEM((4, n, cols), f32)],
        compiler_params=pltpu.CompilerParams(vmem_limit_bytes=VMEM),
        cost_estimate=pl.CostEstimate(flops=2 * n * cols * chans * 8, bytes_accessed=4 * 2**20, transcendentals=0),
        name="norm",
    )(pair, gain, shift, wb)


def proj_kernel(first, xa, xb, w0, w1, w2, w3, *rest):
    if first:
        q_out, sg_out, wo_out, kt_out, v_out, bound, wk_s, wv_s, wq_s, wg_s, gs_s = rest
    else:
        q_in, kt_out, v_out, bound, wk_s, wv_s = rest
    ws = (w0, w1, w2, w3)
    width = 32
    scale = LOG2E / math.sqrt(width)

    @pl.when(pl.program_id(0) == 0)
    def _():
        wts = [w[0:128].astype(f32).T for w in ws]

        def rows(kind):
            return jnp.concatenate([t[kind * width : (kind + 1) * width] for t in wts], axis=0)

        wk_s[...] = rows(1).astype(bf16)
        wv_s[...] = rows(2).T.astype(bf16)
        bound[...] = jnp.zeros_like(bound)
        if first:
            wq_s[...] = rows(0).T.astype(bf16)
            wg_s[...] = rows(3).T.astype(bf16)
            wo_out[...] = jnp.concatenate([w[128:160] for w in ws], axis=0)
            lane = lax.broadcasted_iota(jnp.int32, (1, 128), 1) // width
            total = jnp.zeros((1, 128), f32)
            for h, w in enumerate(ws):
                piece = jnp.sum(w[160:176].astype(f32), axis=0, keepdims=True)
                total = jnp.where(lane == h, piece, total)
            gs_s[...] = jnp.broadcast_to(total, gs_s.shape)

    row = lax.broadcasted_iota(jnp.int32, (128, 128), 0) // width
    col = lax.broadcasted_iota(jnp.int32, (128, 128), 1)
    best = bound[...]
    for ii in range(xa.shape[0]):
        if first:
            q = (dot(xa[ii], wq_s[...]) * scale).astype(bf16)
            q_out[ii] = q
            raw = dot(xa[ii], wg_s[...]).astype(bf16).astype(f32)
            sg_out[ii] = jax.nn.sigmoid(raw + gs_s[0:1])
        else:
            q = q_in[ii]
        high = jnp.zeros((128, 1), f32)
        for t, x in enumerate((xa, xb)):
            kt = dot_nt(wk_s[...], x[ii])
            kt_out[ii, t] = kt.astype(bf16)
            high = jnp.maximum(high, jnp.max(jnp.abs(kt), axis=1, keepdims=True))
            v_out[ii, t] = dot(x[ii], wv_s[...]).astype(bf16)
        spread_k = jnp.where(row == col, high, 0.0).astype(bf16)
        most = dot(jnp.abs(q), spread_k)
        best = jnp.maximum(best, jnp.max(most, axis=0, keepdims=True))
    bound[...] = best


def proj_call(first, xa, xb, ws, q=None):
    n, cols, chans = xa.shape
    per = 4
    block = pl.BlockSpec((per, cols, chans), lambda i: (i, 0, 0))

    def whole(*shape):
        return pl.BlockSpec(shape, lambda i: (0,) * len(shape))

    in_specs = [block, block] + [whole(176, 128)] * 4
    args = [xa, xb, *ws]
    out_specs = [
        pl.BlockSpec((per, 2, chans, cols), lambda i: (i, 0, 0, 0)),
        pl.BlockSpec((per, 2, cols, chans), lambda i: (i, 0, 0, 0)),
        whole(8, 128),
    ]
    out_shape = [
        jax.ShapeDtypeStruct((n, 2, chans, cols), bf16),
        jax.ShapeDtypeStruct((n, 2, cols, chans), bf16),
        jax.ShapeDtypeStruct((8, 128), f32),
    ]
    scratch = [pltpu.VMEM((128, 128), bf16)] * 2
    if first:
        out_specs = [block, block, whole(128, 128)] + out_specs
        out_shape = [
            jax.ShapeDtypeStruct((n, cols, chans), bf16),
            jax.ShapeDtypeStruct((n, cols, chans), f32),
            jax.ShapeDtypeStruct((128, 128), bf16),
        ] + out_shape
        scratch = scratch + [pltpu.VMEM((128, 128), bf16)] * 2 + [pltpu.VMEM((8, 128), f32)]
    else:
        in_specs.append(block)
        args.append(q)
    return pl.pallas_call(
        functools.partial(proj_kernel, first),
        grid=(n // per,),
        in_specs=in_specs,
        out_specs=out_specs,
        out_shape=out_shape,
        scratch_shapes=scratch,
        compiler_params=pltpu.CompilerParams(vmem_limit_bytes=VMEM),
        cost_estimate=pl.CostEstimate(
            flops=2 * n * cols * 2 * 128 * 512, bytes_accessed=10 * 2**20, transcendentals=n * cols * 128
        ),
        name="proj_near" if first else "proj_far",
    )(*args)


def attend_kernel(parts, sc, q, kt_a, kt_b, v_a, v_b, sg, wo, osh, keys, near, far, *rest):
    blocks = rest[: len(parts)]
    out, bias, flag = rest[-3:]
    half = q.shape[1]
    member, yh, z = sc[1], sc[2], sc[3]

    @pl.when(pl.program_id(0) == 0)
    def _():
        most = jnp.zeros((16, 256), f32)
        for block, (place, first_slot) in zip(blocks, parts):
            core = sc[place]
            for slot in range(block.shape[0]):
                zs = (z + (8, 7, 9, 6)[slot + first_slot]) % 8
                for dy in range(2):
                    quarter = (((yh ^ dy) * 2) + core) ^ member
                    for dz in range(2):
                        at = pl.multiple_of((zs ^ (4 * dz)) * 16, 16)
                        for h in range(4):
                            value = block[slot, dy, dz, h].astype(f32) * LOG2E
                            most = jnp.maximum(most, jnp.abs(value))
                            bias[quarter, h ^ member, pl.ds(at, 16), :] = value + keys[quarter]
        reach = jnp.max(most) + jnp.max(jnp.maximum(near[...], far[...]))
        flag[0] = (reach < LIMIT).astype(jnp.int32)

    lane = lax.broadcasted_iota(jnp.int32, (half, 128), 1) // 32
    ones = jnp.ones((256, 128), bf16)

    def keys_of(r):
        return (kt_a, kt_b)[r // 2][0, r % 2]

    def values_of(r):
        return jnp.concatenate([(v_a, v_b)[r // 2][0, r % 2], ones], axis=1)

    def finish(pieces):
        att = jnp.zeros((half, 128), f32)
        for h in range(4):
            att = jnp.where(lane == h, pieces[h][:, :128] / pieces[h][:, 128:], att)
        gated = (att * sg[0]).astype(bf16)
        out[0] = dot(gated, wo[...]) + osh[...]

    def query(h):
        return jnp.where(lane == h, q[0], jnp.zeros_like(q[0]))

    @pl.when(flag[0] == 1)
    def _():
        wide = jnp.concatenate([query(h) for h in range(4)], axis=0)
        acc = None
        for r in range(4):
            s = dot(wide, keys_of(r)) + bias[r].reshape(4 * half, 256)
            p = jnp.exp2(s).astype(bf16)
            part = dot(p, values_of(r))
            acc = part if acc is None else acc + part
        finish([acc[h * half : (h + 1) * half] for h in range(4)])

    @pl.when(flag[0] != 1)
    def _():
        pieces = []
        for h in range(4):
            s = [dot(query(h), keys_of(r)) + bias[r, h] for r in range(4)]
            top = functools.reduce(jnp.maximum, [jnp.max(t, axis=1, keepdims=True) for t in s])
            pieces.append(sum(dot(jnp.exp2(s[r] - top).astype(bf16), values_of(r)) for r in range(4)))
        finish(pieces)


def attend_call(parts, sc, q, kts, vs, sg, wo, osh, keys, bounds, blocks, before, name):
    n, cols, chans = q.shape
    half = cols // 2

    def whole(array):
        rank = array.ndim
        return pl.BlockSpec(array.shape, lambda i, sc: (0,) * rank)

    mine = pl.BlockSpec((1, half, chans), lambda i, sc: (i, sc[0], 0))
    kt_spec = pl.BlockSpec((1, 2, chans, cols), lambda i, sc: (i, 0, 0, 0))
    v_spec = pl.BlockSpec((1, 2, cols, chans), lambda i, sc: (i, 0, 0, 0))
    args = [q, *kts, *vs, sg, wo, osh, keys, *bounds, *blocks]
    in_specs = [mine, kt_spec, kt_spec, v_spec, v_spec, mine] + [whole(a) for a in args[6:]]
    kernel = functools.partial(attend_kernel, parts)
    aliases = {}
    if before is not None:
        args.append(before)
        in_specs.append(pl.BlockSpec(memory_space=pl.ANY))
        aliases = {len(args): 0}
    return pl.pallas_call(
        kernel,
        grid_spec=pltpu.PrefetchScalarGridSpec(
            num_scalar_prefetch=1,
            grid=(n,),
            in_specs=in_specs,
            out_specs=mine,
            scratch_shapes=[pltpu.VMEM((4, 4, half, 256), f32), pltpu.SMEM((1,), jnp.int32)],
        ),
        out_shape=jax.ShapeDtypeStruct((n, cols, chans), f32),
        input_output_aliases=aliases,
        compiler_params=pltpu.CompilerParams(vmem_limit_bytes=VMEM),
        cost_estimate=pl.CostEstimate(
            flops=2 * n * 4 * half * 1024 * 384, bytes_accessed=12 * 2**20, transcendentals=n * 4 * half * 1024
        ),
        name=name,
    )(sc, *args)


def local(pair, token_mask, ln_gain, ln_shift, w_qkvg, w_bias, gate_shift, w_out, out_shift):
    row, member = lax.axis_index("row"), lax.axis_index("head")
    yh, x, z = row // 32, (row // 8) % 4, row % 8

    g_hi = lax.reduce_precision(gate_shift, 8, 7)
    g_mid = lax.reduce_precision(gate_shift - g_hi, 8, 7)
    g_low = gate_shift - g_hi - g_mid
    g_rows = jnp.tile(jnp.stack([g_hi, g_mid, g_low]).astype(bf16), (1, 4))
    pack = jnp.concatenate([w_qkvg, w_out, g_rows, jnp.zeros((13, 128), bf16)], axis=0)
    packs = (pack, send(pack, to_core), send(pack, to_chip), send(pack, to_both))

    wb = jnp.concatenate([w_bias.T, jnp.zeros((12, 128), bf16)], axis=0)
    normed, chunk = norm_call(pair, ln_gain[None], ln_shift[None], wb)

    held = [send(chunk, spread(dy, dz)) for dy in range(2) for dz in range(2)]
    across = send(normed, to_chip)
    beside = send(normed, to_core)
    held = jnp.stack(held).reshape(2, 2, *chunk.shape)
    held = jnp.stack([held, send(held, along_z(1)), send(held, along_z(-1)), send(held, along_z(2))])
    left, right = send(held, along_x(1)), send(held, along_x(-1))
    behind_a, behind_b = send(left[:2], along_x(1)), send(right[2:], along_x(-1))

    q, sg, wo, kt_a, v_a, near = proj_call(True, normed, beside, packs)
    corner = send(across, to_core)
    kt_b, v_b, far = proj_call(False, across, corner, packs, q)

    quarters = jnp.where(token_mask == 1, 0.0, -1e9 * LOG2E).astype(f32).reshape(4, 1, 256)
    keys = jnp.stack([quarters[member ^ r] for r in range(4)])
    lo, hi = (x + 3) % 4, (x + 1) % 4
    common = [member, yh, z]
    osh = out_shift[None]
    sc_a = jnp.stack([1 - x % 2] + common + [lo // 2, hi // 2]).astype(jnp.int32)
    sc_b = jnp.stack([x % 2] + common + [x // 2, 1 - x // 2]).astype(jnp.int32)
    rest = (q, (kt_a, kt_b), (v_a, v_b), sg, wo, osh, keys, (near, far))
    done = attend_call(((4, 0), (5, 0)), sc_a, *rest, (left, right), None, "attend_far")
    return attend_call(
        ((4, 0), (5, 0), (5, 2)), sc_b, *rest, (held, behind_a, behind_b), done, "attend_near"
    )


def solution(mesh):
    placed = (
        P("row", "head", None),
        P(),
        P(),
        P(),
        P(None, "head"),
        P(),
        P("head"),
        P("head", None),
        P(),
    )
    return jax.shard_map(
        local, mesh=mesh, in_specs=placed, out_specs=P("row", "head", None), check_vma=False
    )
```

time: 523 us -> 118 us (0.23)
  matrix products: 179 us -> 0 us
  waiting for transfers between devices: 190 us -> 12.9 us
  local copies, waits for them, and re-layouts: 92.4 us -> 6.77 us
  Pallas kernels: 0 us -> 51.6 us
  starting transfers between devices: 0.12 us -> 45.2 us
  other arithmetic: 35.8 us -> 0.21 us
  between operations: 13.3 us -> 0.12 us
  blocking collectives: 8.76 us -> 0 us
    all_gather x2 -> x0, waiting for transfers between devices: 142 us -> none  [the longest x1 99.2 us: local(): piece = lax.all_gather(head_bias, 'row', axis=0, tiled=True)]
    sub x32 -> x0, matrix products: 96 us -> none  [inner(): weights = jax.nn.softmax(scores, axis=-1).astype(jnp.bfloat16)]
    dot_general x35 -> x0, matrix products: 83.2 us -> none  [the longest x32 74.8 us: inner(): jnp.einsum('ijk,ikc->ijc', weights, values, preferred_element_type=jnp.fl...]
    dynamic_update_slice x32 -> x0, local copies, waits for them, and re-layouts: 72.2 us -> none  [inner(): return lax.dynamic_update_slice_in_dim(acc, part_out, offset, 1)]
    pallas_call x0 -> x5, Pallas kernels: none -> 51.6 us  [the longest x2 36.3 us: attend_call(): pl.pallas_call(kernel, grid_spec=pltpu.PrefetchScalarGridSpec(num_scalar_...]
    reduce_scatter x1 -> x0, waiting for transfers between devices: 48.5 us -> none  [local(): lax.psum_scatter(partial_out.astype(jnp.bfloat16), 'head', scatter_dimens...]
    ppermute x0 -> x17, starting transfers between devices: none -> 45.2 us  [send(): return lax.ppermute(value, ('row', 'head'), pairs)]
    convert_element_type x33 -> x0, other arithmetic: 29.4 us -> none  [the longest x32 27.4 us: inner(): lax.dynamic_slice_in_dim(piece, offset, step_rows, 0).astype(jnp.float32)]
  transfers between devices with their start and end apart: 3 -> 17, of which waited for: 3 -> 4; matrix products, arithmetic and copies ran while one was open for 4% -> 1% of each run, Pallas kernels for 0% -> 26%
where the time goes in v1:
time: 118 us; the launch traced here: 117 us
  Pallas kernels  51.6 us (44%)
  starting transfers between devices  45.2 us (38%)
  waiting for transfers between devices  12.9 us (11%)
  local copies, waits for them, and re-layouts  6.77 us (6%)
    ppermute x17, starting transfers between devices, send(): return lax.ppermute(value, ('row', 'head'), pairs)  45.2 us
    pallas_call x2, Pallas kernels, attend_call(): pl.pallas_call(kernel, grid_spec=pltpu.PrefetchScalarGridSpec(num_scalar_...  36.3 us
    ppermute x17, waiting for transfers between devices, send(): return lax.ppermute(value, ('row', 'head'), pairs)  12.9 us
    pallas_call x2, Pallas kernels, proj_call(): pl.pallas_call(functools.partial(proj_kernel, first), grid=(n // per,), i...  12.4 us
    unnamed x22, local copies, waits for them, and re-layouts  5.67 us
    pallas_call x1, Pallas kernels, norm_call(): pl.pallas_call(norm_kernel, grid=(n // per,), in_specs=[pl.BlockSpec((per...  2.88 us
  transfers between devices with their start and end apart: 17, of which 4 were waited for; matrix products, arithmetic and copies ran while one was open for 1% of the time, Pallas kernels for 26%

profile of v1, /device:TPU:1, one launch (start us, length us, event | category | flops | bytes accessed | tf_op | source)
XLA Modules:
  0.0 116.8 jit_solution(16766888157920999008)
XLA Ops:
  0.0 0.7 concatenate.11.wb
  0.7 1.6 %copy-done = f32[16,256,128]{2,1,0:T(8,128)S(1)} copy-done((f32[16,256,128]{2,1,0:T(8,128)S(1)}, f32[16,256,128]{2,1,0:T(8,128)}, u32[]{:S(2)}) %copy-start) | copy-done | bytes 2097176
  2.3 0.7 copy-done.1
  3.6 2.9 %norm.1 = (bf16[16,256,128]{2,1,0:T(8,128)(2,1)}, bf16[4,16,256]{2,1,0:T(8,128)(2,1)S(1)}) custom-call(f32[16,256,128]{2,1,0:T(8,128)S(1)} %copy-done, f32[1,128]{1,0:T(1,128)S(1)} %bitcast.29, f32[1,128]{1,0:T(1,128)S(1)} %bitcast.30, bf16[16,128]{1,0:T(8,128)(2,1)S(1)} %concatenate.11.wb), custom_call_target="tpu_custom_call" | custom-call | flops 8388608 | bytes 4194304 | tf_op jit(solution)/shard_map/norm/pallas_call | solution.py:93
  6.5 2.1 %collective-permute-start.4 = (bf16[16,256,128]{2,1,0:T(8,128)(2,1)}, bf16[16,256,128]{2,1,0:T(8,128)(2,1)S(1)}, u32[]{:S(2)}, u32[]{:S(2)}) collective-permute-start(bf16[16,256,128]{2,1,0:T(8,128)(2,1)} %get-tuple-element.16.xa), channel_id=1, source_target_pairs={{0,2},{1,3},{2,0},{3,1},{4,6},{5,7},{6,4},{7,5},{8,10},{9,11},{10,... | collective-permute-start | bytes 3145736 | tf_op jit(solution)/shard_map/ppermute | solution.py:33
  8.6 12.5 %collective-permute-start.9 = (bf16[4,16,256]{2,1,0:T(8,128)(2,1)S(1)}, bf16[4,16,256]{2,1,0:T(8,128)(2,1)S(1)}, u32[]{:S(2)}, u32[]{:S(2)}) collective-permute-start(bf16[4,16,256]{2,1,0:T(8,128)(2,1)S(1)} %get-tuple-element.26), channel_id=1, source_target_pairs={{0,144},{1,208},{2,16},{3,80},{4,148},{5,212},{6,20},{7,84},{8,152... | collective-permute-start | bytes 98312 | tf_op jit(solution)/shard_map/ppermute | solution.py:33
  21.2 1.6 %collective-permute-start.7 = (bf16[4,16,256]{2,1,0:T(8,128)(2,1)S(1)}, bf16[4,16,256]{2,1,0:T(8,128)(2,1)S(1)}, u32[]{:S(2)}, u32[]{:S(2)}) collective-permute-start(bf16[4,16,256]{2,1,0:T(8,128)(2,1)S(1)} %get-tuple-element.26), channel_id=1, source_target_pairs={{0,16},{1,80},{2,144},{3,208},{4,20},{5,84},{6,148},{7,212},{8,24}... | collective-permute-start | bytes 98312 | tf_op jit(solution)/shard_map/ppermute | solution.py:33
  22.8 3.7 %collective-permute-start.6 = (bf16[4,16,256]{2,1,0:T(8,128)(2,1)S(1)}, bf16[4,16,256]{2,1,0:T(8,128)(2,1)S(1)}, u32[]{:S(2)}, u32[]{:S(2)}) collective-permute-start(bf16[4,16,256]{2,1,0:T(8,128)(2,1)S(1)} %get-tuple-element.26), channel_id=1, source_target_pairs={{0,0},{1,64},{2,128},{3,192},{4,4},{5,68},{6,132},{7,196},{8,8},{9... | collective-permute-start | bytes 98312 | tf_op jit(solution)/shard_map/ppermute | solution.py:33
  27.2 3.6 %collective-permute-done.7 = bf16[4,16,256]{2,1,0:T(8,128)(2,1)S(1)} collective-permute-done((bf16[4,16,256]{2,1,0:T(8,128)(2,1)S(1)}, bf16[4,16,256]{2,1,0:T(8,128)(2,1)S(1)}, u32[]{:S(2)}, u32[]{:S(2)}) %collective-permute-start.7) | collective-permute-done | bytes 32800 | tf_op jit(solution)/shard_map/ppermute | solution.py:33
  30.9 1.7 %collective-permute-start.12 = (bf16[2,2,4,16,256]{4,3,2,1,0:T(8,128)(2,1)S(1)}, bf16[2,2,4,16,256]{4,3,2,1,0:T(8,128)(2,1)S(1)}, u32[]{:S(2)}, u32[]{:S(2)}) collective-permute-start(bf16[2,2,4,16,256]{4,3,2,1,0:T(8,128)(2,1)S(1)} %bitcast.33), channel_id=1, source_target_pairs={{0,8},{1,9},{2,10},{3,11},{4,12},{5,13},{6,14},{7,15},{8,16},{9,17... | collective-permute-start | bytes 393224 | tf_op jit(solution)/shard_map/ppermute | solution.py:33
  32.6 2.7 %collective-permute-start.11 = (bf16[2,2,4,16,256]{4,3,2,1,0:T(8,128)(2,1)S(1)}, bf16[2,2,4,16,256]{4,3,2,1,0:T(8,128)(2,1)S(1)}, u32[]{:S(2)}, u32[]{:S(2)}) collective-permute-start(bf16[2,2,4,16,256]{4,3,2,1,0:T(8,128)(2,1)S(1)} %bitcast.34), channel_id=1, source_target_pairs={{0,28},{1,29},{2,30},{3,31},{4,0},{5,1},{6,2},{7,3},{8,4},{9,5},{1... | collective-permute-start | bytes 393224 | tf_op jit(solution)/shard_map/ppermute | solution.py:33
  35.3 5.3 %collective-permute-start.5 = (bf16[16,256,128]{2,1,0:T(8,128)(2,1)S(1)}, bf16[16,256,128]{2,1,0:T(8,128)(2,1)}, u32[]{:S(2)}, u32[]{:S(2)}) collective-permute-start(bf16[16,256,128]{2,1,0:T(8,128)(2,1)S(1)} %collective-permute-done.4.xa), channel_id=1, source_target_pairs={{0,1},{1,0},{2,3},{3,2},{4,5},{5,4},{6,7},{7,6},{8,9},{9,8},{10,11... | collective-permute-start | bytes 3145736 | tf_op jit(solution)/shard_map/ppermute | solution.py:33
  40.9 6.9 %collective-permute-start.15 = (bf16[4,2,2,4,16,256]{5,4,3,2,1,0:T(8,128)(2,1)S(1)}, bf16[4,2,2,4,16,256]{5,4,3,2,1,0:T(8,128)(2,1)S(1)}, u32[]{:S(2)}, u32[]{:S(2)}) collective-permute-start(bf16[4,2,2,4,16,256]{5,4,3,2,1,0:T(8,128)(2,1)S(1)} %pad_maximum_fusion.rest_0_), channel_id=1, source_target_pairs={{0,96},{1,97},{2,98},{3,99},{4,100},{5,101},{6,102},{7,103},{8,104... | collective-permute-start | bytes 1572872 | tf_op jit(solution)/shard_map/ppermute | solution.py:33
  47.9 3.5 %collective-permute-start.3 = (bf16[176,128]{1,0:T(8,128)(2,1)S(1)}, bf16[176,128]{1,0:T(8,128)(2,1)S(1)}, u32[]{:S(2)}, u32[]{:S(2)}) collective-permute-start(bf16[176,128]{1,0:T(8,128)(2,1)S(1)} %maximum_maximum_fusion.w0), channel_id=1, source_target_pairs={{0,3},{1,2},{2,1},{3,0},{4,7},{5,6},{6,5},{7,4},{8,11},{9,10},{10,... | collective-permute-start | bytes 135176 | tf_op jit(solution)/shard_map/ppermute | solution.py:33
  51.3 7.5 %collective-permute-done.15.rest_1_ = bf16[4,2,2,4,16,256]{5,4,3,2,1,0:T(8,128)(2,1)S(1)} collective-permute-done((bf16[4,2,2,4,16,256]{5,4,3,2,1,0:T(8,128)(2,1)S(1)}, bf16[4,2,2,4,16,256]{5,4,3,2,1,0:T(8,128)(2,1)S(1)}, u32[]{:S(2)}, u32[]{:S(2)}) %collective-permute-start.15) | collective-permute-done | bytes 524320 | tf_op jit(solution)/shard_map/ppermute | solution.py:33
  58.9 2.3 %collective-permute-start.2 = (bf16[176,128]{1,0:T(8,128)(2,1)S(1)}, bf16[176,128]{1,0:T(8,128)(2,1)S(1)}, u32[]{:S(2)}, u32[]{:S(2)}) collective-permute-start(bf16[176,128]{1,0:T(8,128)(2,1)S(1)} %maximum_maximum_fusion.w0), channel_id=1, source_target_pairs={{0,2},{1,3},{2,0},{3,1},{4,6},{5,7},{6,4},{7,5},{8,10},{9,11},{10,... | collective-permute-start | bytes 135176 | tf_op jit(solution)/shard_map/ppermute | solution.py:33
  61.1 1.2 %collective-permute-done.13.rest_0_ = bf16[4,2,2,4,16,256]{5,4,3,2,1,0:T(8,128)(2,1)S(1)} collective-permute-done((bf16[4,2,2,4,16,256]{5,4,3,2,1,0:T(8,128)(2,1)S(1)}, bf16[4,2,2,4,16,256]{5,4,3,2,1,0:T(8,128)(2,1)S(1)}, u32[]{:S(2)}, u32[]{:S(2)}) %collective-permute-start.13) | collective-permute-done | bytes 524320 | tf_op jit(solution)/shard_map/ppermute | solution.py:33
  62.9 2.3 %collective-permute-start.16 = (bf16[2,2,2,4,16,256]{5,4,3,2,1,0:T(8,128)(2,1)S(1)}, bf16[2,2,2,4,16,256]{5,4,3,2,1,0:T(8,128)(2,1)S(1)}, u32[]{:S(2)}, u32[]{:S(2)}) collective-permute-start(bf16[2,2,2,4,16,256]{5,4,3,2,1,0:T(8,128)(2,1)S(1)} %slice.9), channel_id=1, source_target_pairs={{0,96},{1,97},{2,98},{3,99},{4,100},{5,101},{6,102},{7,103},{8,104... | collective-permute-start | bytes 786440 | tf_op jit(solution)/shard_map/ppermute | solution.py:33
  65.3 6.5 %proj_near.1 = (bf16[16,256,128]{2,1,0:T(8,128)(2,1)S(1)}, f32[16,256,128]{2,1,0:T(8,128)S(1)}, bf16[128,128]{1,0:T(8,128)(2,1)S(1)}, bf16[16,2,128,256]{3,2,1,0...) custom-call(bf16[16,256,128]{2,1,0:T(8,128)(2,1)} %get-tuple-element.16.xa, ...), custom_call_target="tpu_custom_call" | custom-call | flops 1073741824 | bytes 10485760 | tf_op jit(solution)/shard_map/proj_near/pallas_call | solution.py:202
  71.8 1.4 %copy-done.5 = f32[16,256,128]{2,1,0:T(8,128)} copy-done((f32[16,256,128]{2,1,0:T(8,128)}, f32[16,256,128]{2,1,0:T(8,128)S(1)}, u32[]{:S(2)}) %copy-start.5) | copy-done | bytes 2097176
  73.1 6.0 %proj_far.1 = (bf16[16,2,128,256]{3,2,1,0:T(8,128)(2,1)S(1)}, bf16[16,2,256,128]{3,2,1,0:T(8,128)(2,1)}, f32[8,128]{1,0:T(8,128)S(1)}) custom-call(bf16[16,256,128]{2,1,0:T(8,128)(2,1)S(1)} %collective-permute-done.4.xa, bf16[16,256,128]{2,1,0:T(8,128)(2,1)} %collective-permute-done.5.xb, bf16[176,128]{1,0:T(8,128)(2,1)S(1)} %maximum_maximum_fusion.w0, ...), custom_call_target="tpu_custom_call" | custom-call | flops 1073741824 | bytes 10485760 | tf_op jit(solution)/shard_map/proj_far/pallas_call | solution.py:202
  79.1 1.4 %copy-done.4 = bf16[16,2,128,256]{3,2,1,0:T(8,128)(2,1)} copy-done((bf16[16,2,128,256]{3,2,1,0:T(8,128)(2,1)}, bf16[16,2,128,256]{3,2,1,0:T(8,128)(2,1)S(1)}, u32[]{:S(2)}) %copy-start.4) | copy-done | bytes 2097176
  80.5 18.1 %attend_far.1.rest_3_ = f32[16,256,128]{2,1,0:T(8,128)} custom-call(s32[6]{0:T(128)S(1)} %stack.102.sc, bf16[16,256,128]{2,1,0:T(8,128)(2,1)S(1)} %get-tuple-element.17.rest_0_.q, bf16[16,2,128,256]{3,2,1,0:T(8,128)(2,1)S(1)} %copy-done.6, bf16[16,2,128,256]{3,2,1,0:T(8,128)(2,1)} %copy-done.4, bf16[16,2,256,128]{3,2,1,0:T(8,128)(2,1)} %get-tuple-element.20.v_a, ...), custom_call_target="tpu_custom_call" | custom-call | flops 6442450944 | bytes 12582912 | tf_op jit(solution)/shard_map/attend_far/pallas_call | solution.py:300
  98.6 18.2 %attend_near.1 = f32[16,256,128]{2,1,0:T(8,128)} custom-call(s32[6]{0:T(128)S(1)} %stack.84.sc, bf16[16,256,128]{2,1,0:T(8,128)(2,1)S(1)} %get-tuple-element.17.rest_0_.q, bf16[16,2,128,256]{3,2,1,0:T(8,128)(2,1)S(1)} %copy-done.6, bf16[16,2,128,256]{3,2,1,0:T(8,128)(2,1)} %copy-done.4, ...), custom_call_target="tpu_custom_call", output_to_operand_aliasing={{}: (15, {})} | custom-call | flops 6442450944 | bytes 12582912 | tf_op jit(solution)/shard_map/attend_near/pallas_call | solution.py:300
  (54 shorter events, 2.4 us)
Async XLA Ops:
  0.0 40.6 %copy-start.10 = (f32[32]{0:T(128)S(1)}, f32[32]{0:T(128)}, u32[]{:S(2)}) copy-start(f32[32]{0:T(128)} %param.15) | copy-start | bytes 388
  0.0 47.8 %copy-start.8 = (bf16[32,128]{1,0:T(8,128)(2,1)S(1)}, bf16[32,128]{1,0:T(8,128)(2,1)}, u32[]{:S(2)}) copy-start(bf16[32,128]{1,0:T(8,128)(2,1)} %param.16) | copy-start | bytes 24580
  0.7 1.6 %copy-start = (f32[16,256,128]{2,1,0:T(8,128)S(1)}, f32[16,256,128]{2,1,0:T(8,128)}, u32[]{:S(2)}) copy-start(f32[16,256,128]{2,1,0:T(8,128)} %pair.1) | copy-start | bytes 6291460
  3.6 44.1 %copy-start.7 = (bf16[128,128]{1,0:T(8,128)(2,1)S(1)}, bf16[128,128]{1,0:T(8,128)(2,1)}, u32[]{:S(2)}) copy-start(bf16[128,128]{1,0:T(8,128)(2,1)} %param.13) | copy-start | bytes 98308
  3.6 47.7 %copy-start.9 = (s32[1024]{0:T(1024)S(1)}, s32[1024]{0:T(1024)}, u32[]{:S(2)}) copy-start(s32[1024]{0:T(1024)} %param.10) | copy-start | bytes 12292
  6.5 28.8 %collective-permute-start.4 = (bf16[16,256,128]{2,1,0:T(8,128)(2,1)}, bf16[16,256,128]{2,1,0:T(8,128)(2,1)S(1)}, u32[]{:S(2)}, u32[]{:S(2)}) collective-permute-start(bf16[16,256,128]{2,1,0:T(8,128)(2,1)} %get-tuple-element.16.xa), channel_id=1, source_target_pairs={{0,2},{1,3},{2,0},{3,1},{4,6},{5,7},{6,4},{7,5},{8,10},{9,11},{10,... | collective-permute-start | bytes 3145736 | tf_op jit(solution)/shard_map/ppermute | solution.py:33
  8.6 17.9 %collective-permute-start.9 = (bf16[4,16,256]{2,1,0:T(8,128)(2,1)S(1)}, bf16[4,16,256]{2,1,0:T(8,128)(2,1)S(1)}, u32[]{:S(2)}, u32[]{:S(2)}) collective-permute-start(bf16[4,16,256]{2,1,0:T(8,128)(2,1)S(1)} %get-tuple-element.26), channel_id=1, source_target_pairs={{0,144},{1,208},{2,16},{3,80},{4,148},{5,212},{6,20},{7,84},{8,152... | collective-permute-start | bytes 98312 | tf_op jit(solution)/shard_map/ppermute | solution.py:33
  21.2 6.0 %collective-permute-start.8 = (bf16[4,16,256]{2,1,0:T(8,128)(2,1)S(1)}, bf16[4,16,256]{2,1,0:T(8,128)(2,1)S(1)}, u32[]{:S(2)}, u32[]{:S(2)}) collective-permute-start(bf16[4,16,256]{2,1,0:T(8,128)(2,1)S(1)} %get-tuple-element.26), channel_id=1, source_target_pairs={{0,128},{1,192},{2,0},{3,64},{4,132},{5,196},{6,4},{7,68},{8,136},... | collective-permute-start | bytes 98312 | tf_op jit(solution)/shard_map/ppermute | solution.py:33
  21.2 9.7 %collective-permute-start.7 = (bf16[4,16,256]{2,1,0:T(8,128)(2,1)S(1)}, bf16[4,16,256]{2,1,0:T(8,128)(2,1)S(1)}, u32[]{:S(2)}, u32[]{:S(2)}) collective-permute-start(bf16[4,16,256]{2,1,0:T(8,128)(2,1)S(1)} %get-tuple-element.26), channel_id=1, source_target_pairs={{0,16},{1,80},{2,144},{3,208},{4,20},{5,84},{6,148},{7,212},{8,24}... | collective-permute-start | bytes 98312 | tf_op jit(solution)/shard_map/ppermute | solution.py:33
  22.8 8.0 %collective-permute-start.6 = (bf16[4,16,256]{2,1,0:T(8,128)(2,1)S(1)}, bf16[4,16,256]{2,1,0:T(8,128)(2,1)S(1)}, u32[]{:S(2)}, u32[]{:S(2)}) collective-permute-start(bf16[4,16,256]{2,1,0:T(8,128)(2,1)S(1)} %get-tuple-element.26), channel_id=1, source_target_pairs={{0,0},{1,64},{2,128},{3,192},{4,4},{5,68},{6,132},{7,196},{8,8},{9... | collective-permute-start | bytes 98312 | tf_op jit(solution)/shard_map/ppermute | solution.py:33
  26.5 38.8 %collective-permute-start = (bf16[16,256,128]{2,1,0:T(8,128)(2,1)}, bf16[16,256,128]{2,1,0:T(8,128)(2,1)}, u32[]{:S(2)}, u32[]{:S(2)}) collective-permute-start(bf16[16,256,128]{2,1,0:T(8,128)(2,1)} %get-tuple-element.16.xa), channel_id=1, source_target_pairs={{0,1},{1,0},{2,3},{3,2},{4,5},{5,4},{6,7},{7,6},{8,9},{9,8},{10,11... | collective-permute-start | bytes 3145736 | tf_op jit(solution)/shard_map/ppermute | solution.py:33
  30.9 9.9 %collective-permute-start.12 = (bf16[2,2,4,16,256]{4,3,2,1,0:T(8,128)(2,1)S(1)}, bf16[2,2,4,16,256]{4,3,2,1,0:T(8,128)(2,1)S(1)}, u32[]{:S(2)}, u32[]{:S(2)}) collective-permute-start(bf16[2,2,4,16,256]{4,3,2,1,0:T(8,128)(2,1)S(1)} %bitcast.33), channel_id=1, source_target_pairs={{0,8},{1,9},{2,10},{3,11},{4,12},{5,13},{6,14},{7,15},{8,16},{9,17... | collective-permute-start | bytes 393224 | tf_op jit(solution)/shard_map/ppermute | solution.py:33
  32.6 8.2 %collective-permute-start.11 = (bf16[2,2,4,16,256]{4,3,2,1,0:T(8,128)(2,1)S(1)}, bf16[2,2,4,16,256]{4,3,2,1,0:T(8,128)(2,1)S(1)}, u32[]{:S(2)}, u32[]{:S(2)}) collective-permute-start(bf16[2,2,4,16,256]{4,3,2,1,0:T(8,128)(2,1)S(1)} %bitcast.34), channel_id=1, source_target_pairs={{0,28},{1,29},{2,30},{3,31},{4,0},{5,1},{6,2},{7,3},{8,4},{9,5},{1... | collective-permute-start | bytes 393224 | tf_op jit(solution)/shard_map/ppermute | solution.py:33
  35.3 5.5 %collective-permute-start.10 = (bf16[2,2,4,16,256]{4,3,2,1,0:T(8,128)(2,1)S(1)}, bf16[2,2,4,16,256]{4,3,2,1,0:T(8,128)(2,1)S(1)}, u32[]{:S(2)}, u32[]{:S(2)}) collective-permute-start(bf16[2,2,4,16,256]{4,3,2,1,0:T(8,128)(2,1)S(1)} %bitcast.35), channel_id=1, source_target_pairs={{0,4},{1,5},{2,6},{3,7},{4,8},{5,9},{6,10},{7,11},{8,12},{9,13},{1... | collective-permute-start | bytes 393224 | tf_op jit(solution)/shard_map/ppermute | solution.py:33
  35.3 37.9 %collective-permute-start.5 = (bf16[16,256,128]{2,1,0:T(8,128)(2,1)S(1)}, bf16[16,256,128]{2,1,0:T(8,128)(2,1)}, u32[]{:S(2)}, u32[]{:S(2)}) collective-permute-start(bf16[16,256,128]{2,1,0:T(8,128)(2,1)S(1)} %collective-permute-done.4.xa), channel_id=1, source_target_pairs={{0,1},{1,0},{2,3},{3,2},{4,5},{5,4},{6,7},{7,6},{8,9},{9,8},{10,11... | collective-permute-start | bytes 3145736 | tf_op jit(solution)/shard_map/ppermute | solution.py:33
  40.9 18.0 %collective-permute-start.15 = (bf16[4,2,2,4,16,256]{5,4,3,2,1,0:T(8,128)(2,1)S(1)}, bf16[4,2,2,4,16,256]{5,4,3,2,1,0:T(8,128)(2,1)S(1)}, u32[]{:S(2)}, u32[]{:S(2)}) collective-permute-start(bf16[4,2,2,4,16,256]{5,4,3,2,1,0:T(8,128)(2,1)S(1)} %pad_maximum_fusion.rest_0_), channel_id=1, source_target_pairs={{0,96},{1,97},{2,98},{3,99},{4,100},{5,101},{6,102},{7,103},{8,104... | collective-permute-start | bytes 1572872 | tf_op jit(solution)/shard_map/ppermute | solution.py:33
  47.8 14.6 %collective-permute-start.13 = (bf16[4,2,2,4,16,256]{5,4,3,2,1,0:T(8,128)(2,1)S(1)}, bf16[4,2,2,4,16,256]{5,4,3,2,1,0:T(8,128)(2,1)S(1)}, u32[]{:S(2)}, u32[]{:S(2)}) collective-permute-start(bf16[4,2,2,4,16,256]{5,4,3,2,1,0:T(8,128)(2,1)S(1)} %pad_maximum_fusion.rest_0_), channel_id=1, source_target_pairs={{0,32},{1,33},{2,34},{3,35},{4,36},{5,37},{6,38},{7,39},{8,40},{9,... | collective-permute-start | bytes 1572872 | tf_op jit(solution)/shard_map/ppermute | solution.py:33
  47.9 15.1 %collective-permute-start.3 = (bf16[176,128]{1,0:T(8,128)(2,1)S(1)}, bf16[176,128]{1,0:T(8,128)(2,1)S(1)}, u32[]{:S(2)}, u32[]{:S(2)}) collective-permute-start(bf16[176,128]{1,0:T(8,128)(2,1)S(1)} %maximum_maximum_fusion.w0), channel_id=1, source_target_pairs={{0,3},{1,2},{2,1},{3,0},{4,7},{5,6},{6,5},{7,4},{8,11},{9,10},{10,... | collective-permute-start | bytes 135176 | tf_op jit(solution)/shard_map/ppermute | solution.py:33
  58.9 6.4 %collective-permute-start.2 = (bf16[176,128]{1,0:T(8,128)(2,1)S(1)}, bf16[176,128]{1,0:T(8,128)(2,1)S(1)}, u32[]{:S(2)}, u32[]{:S(2)}) collective-permute-start(bf16[176,128]{1,0:T(8,128)(2,1)S(1)} %maximum_maximum_fusion.w0), channel_id=1, source_target_pairs={{0,2},{1,3},{2,0},{3,1},{4,6},{5,7},{6,4},{7,5},{8,10},{9,11},{10,... | collective-permute-start | bytes 135176 | tf_op jit(solution)/shard_map/ppermute | solution.py:33
  62.3 3.0 %collective-permute-start.1 = (bf16[176,128]{1,0:T(8,128)(2,1)S(1)}, bf16[176,128]{1,0:T(8,128)(2,1)S(1)}, u32[]{:S(2)}, u32[]{:S(2)}) collective-permute-start(bf16[176,128]{1,0:T(8,128)(2,1)S(1)} %maximum_maximum_fusion.w0), channel_id=1, source_target_pairs={{0,1},{1,0},{2,3},{3,2},{4,5},{5,4},{6,7},{7,6},{8,9},{9,8},{10,11... | collective-permute-start | bytes 135176 | tf_op jit(solution)/shard_map/ppermute | solution.py:33
  62.9 35.7 %collective-permute-start.16 = (bf16[2,2,2,4,16,256]{5,4,3,2,1,0:T(8,128)(2,1)S(1)}, bf16[2,2,2,4,16,256]{5,4,3,2,1,0:T(8,128)(2,1)S(1)}, u32[]{:S(2)}, u32[]{:S(2)}) collective-permute-start(bf16[2,2,2,4,16,256]{5,4,3,2,1,0:T(8,128)(2,1)S(1)} %slice.9), channel_id=1, source_target_pairs={{0,96},{1,97},{2,98},{3,99},{4,100},{5,101},{6,102},{7,103},{8,104... | collective-permute-start | bytes 786440 | tf_op jit(solution)/shard_map/ppermute | solution.py:33
  65.3 33.3 %collective-permute-start.14 = (bf16[2,2,2,4,16,256]{5,4,3,2,1,0:T(8,128)(2,1)S(1)}, bf16[2,2,2,4,16,256]{5,4,3,2,1,0:T(8,128)(2,1)S(1)}, u32[]{:S(2)}, u32[]{:S(2)}) collective-permute-start(bf16[2,2,2,4,16,256]{5,4,3,2,1,0:T(8,128)(2,1)S(1)} %slice.8), channel_id=1, source_target_pairs={{0,32},{1,33},{2,34},{3,35},{4,36},{5,37},{6,38},{7,39},{8,40},{9,... | collective-permute-start | bytes 786440 | tf_op jit(solution)/shard_map/ppermute | solution.py:33
  73.1 7.4 %copy-start.3 = (f32[128]{0:T(128)S(1)}, f32[128]{0:T(128)}, u32[]{:S(2)}) copy-start(f32[128]{0:T(128)} %param.17) | copy-start | bytes 1540
  73.1 7.4 %copy-start.6 = (bf16[16,2,128,256]{3,2,1,0:T(8,128)(2,1)S(1)}, bf16[16,2,128,256]{3,2,1,0:T(8,128)(2,1)}, u32[]{:S(2)}) copy-start(bf16[16,2,128,256]{3,2,1,0:T(8,128)(2,1)} %get-tuple-element.18.kt_a) | copy-start | bytes 6291460
  (4 other events, 4.1 us)
